TPU v7x, 32 devices: a whole 2x2x4 slice. The times are simulated.
32 devices in a mesh: groups: 2 (over y), dp: 4 (over x, core), query: 4 (over z).
Axes of the slice: x: 2, y: 2, z: 4, core: 2. Of those that a mesh axis runs over, the one named last changes fastest.
Arguments:
- hidden: bfloat16 [8192, 14336], P(('groups', 'dp', 'query')), parts along dimension 0, may hold values from -6 to 6
- out_grad: bfloat16 [8192, 4096], P(('groups', 'dp', 'query')), parts along dimension 0, may hold values from -6 to 6
- doc_ids: int32 [8192], P(('groups', 'dp', 'query')), parts along dimension 0, may hold values from 0 to 255, as said below
- proj_in: bfloat16 [64, 14336], replicated, may hold values from -0.046875 to 0.046875
- proj_out: bfloat16 [64, 4096], replicated, may hold values from -0.09375 to 0.09375
- query_grads: bfloat16 [384, 4096], P(('dp', 'query')), may hold values from -0.0234375 to 0.0234375
Outputs:
- scores: float32 [384, 512], P(('dp', 'query'), 'groups'), parts along dimension 1
There are 2 independent parts, one for each index of `groups`. A program takes and returns all parts, laid end to end along the dimension named above; an argument that names none is the same for every part. Nothing has to cross between parts.
Inputs may be any that keep to these rules, and one draw needn't show every extreme that they name: `doc_ids`: never falling along the tokens. The tokens of each device (aligned blocks of 256) hold the last tokens of exactly 16 documents; the first token starts document 0 and the last token ends document 256 - 1.
All inputs are finite; a program needn't handle non-finite values.
Results may differ from a plain program's by a relative error of at most 0.005.
Values may be sent and summed in bfloat16 or wider, within the bound.
A program may use at most 128 MiB of HBM per device.

v0:
```python
import jax
import jax.numpy as jnp
from jax import lax
from jax.sharding import PartitionSpec as P

DOC_DEV = 16


def passed_along(x, axis, by):
    count = lax.axis_size(axis)
    pairs = [(i, i + by) for i in range(count) if 0 <= i + by < count]
    return lax.ppermute(x, axis, pairs)


def on_device(hidden, out_grad, doc_ids, proj_in, proj_out, query_grads):
    contract = (((1,), (1,)), ((), ()))
    tokens_here = hidden.shape[0]
    width = proj_in.shape[0]
    slots = DOC_DEV + 1
    in_factor = lax.dot_general(
        hidden, proj_in, contract, preferred_element_type=jnp.float32
    ).astype(jnp.bfloat16)
    out_factor = lax.dot_general(
        out_grad, proj_out, contract, preferred_element_type=jnp.float32
    ).astype(jnp.bfloat16)
    local_doc = doc_ids - doc_ids[0]
    member = local_doc[:, None] == jnp.arange(slots, dtype=jnp.int32)[None, :]
    spread = jnp.where(member[:, :, None], out_factor[:, None, :], jnp.zeros((), jnp.bfloat16))
    spread = spread.reshape(tokens_here, slots * width)
    partial_value = lax.dot_general(
        spread, in_factor, (((0,), (0,)), ((), ())), preferred_element_type=jnp.float32
    )
    partial_value = partial_value.reshape(slots, width * width)
    incoming = passed_along(partial_value[DOC_DEV], ("dp", "query"), 1)
    owned = jnp.concatenate(
        [partial_value[0:1] + incoming[None, :], partial_value[1:DOC_DEV]], axis=0
    ).astype(jnp.bfloat16)
    return lax.dot_general(
        query_grads,
        lax.all_gather(owned, ("dp", "query"), axis=0, tiled=True),
        contract,
        preferred_element_type=jnp.float32,
    )


def solution(mesh):
    placed = (
        P(("groups", "dp", "query"), None),
        P(("groups", "dp", "query"), None),
        P(("groups", "dp", "query")),
        P(),
        P(),
        P(("dp", "query"), None),
    )
    return jax.shard_map(
        on_device,
        mesh=mesh,
        in_specs=placed,
        out_specs=P(("dp", "query"), "groups"),
        check_vma=False,
    )
```

profile of v0, /device:TPU:0, one launch (start us, length us, event | category | flops | bytes accessed | tf_op | source)
XLA Modules:
  0.0 77.7 jit_solution(15497180108067892669)
XLA Ops:
  6.5 0.0 copy-start
  6.5 0.0 all-gather.2.cloned.1.call-start
  6.5 1.3 %slice.20 = s32[1]{0:T(128)} slice(s32[256]{0:T(256)} %param.8), slice={[0:1]} | slice | bytes 8 | tf_op jit(solution)/shard_map/slice | solution.py:26
  7.9 1.3 %broadcast_subtract_fusion = s32[256]{0:T(256)S(1)} fusion(s32[256]{0:T(256)} %param.8, s32[]{:T(128)} %bitcast), kind=kLoop, calls=%fused_computation.9 | loop fusion | flops 256 | bytes 2052 | tf_op jit(solution)/shard_map/sub | solution.py:26
  9.2 0.0 copy-done
  9.2 1.8 %convolution_convert_fusion.1 = bf16[256,64]{0,1:T(8,128)(2,1)S(1)} fusion(bf16[256,4096]{1,0:T(8,128)(2,1)S(1)} %copy-done, bf16[64,4096]{1,0:T(8,128)(2,1)} %param.10), kind=kOutput, calls=%fused_computation.2 | convolution fusion | flops 134234112 | bytes 2654208 | tf_op jit(solution)/shard_map/dot_general | solution.py:23
  11.1 0.0 copy-start.1
  11.1 6.2 %fusion = f32[1088,64]{0,1:T(8,128)S(1)} fusion(bf16[256,1088]{0,1:T(8,128)(2,1)S(1)} %bitcast.11, bf16[256,14336]{1,0:T(8,128)(2,1)} %param.6, bf16[64,14336]{1,0:T(8,128)(2,1)} %param.9), kind=kOutput, calls=%fused_computation.1 | convolution fusion | flops 505430016 | bytes 10010624 | tf_op jit(solution)/shard_map/dot_general | solution.py:30
  17.3 0.1 copy.9
  17.4 0.1 squeeze.7
  17.4 4.9 %collective-permute-start = (f32[4096]{0:T(1024)S(1)}, f32[4096]{0:T(1024)S(1)}, u32[]{:S(2)}, u32[]{:S(2)}) collective-permute-start(f32[4096]{0:T(1024)S(1)} %squeeze.7), channel_id=1, source_target_pairs={{0,1},{1,2},{2,3},{3,4},{4,5},{5,6},{6,7},{7,8},{8,9},{9,10},{10,1... | collective-permute-start | bytes 49160 | tf_op jit(solution)/shard_map/ppermute | solution.py:12
  22.4 0.1 slice.30
  22.5 0.1 copy.8
  22.6 0.1 slice.22
  22.6 0.2 copy.10
  22.8 0.2 slice.25
  23.1 0.7 collective-permute-done
  23.8 0.7 pad_maximum_fusion
  24.5 0.0 all-gather.2.cloned.1.call-update
  24.6 43.5 %all-gather.2.cloned.1.call-done = bf16[256,4096]{1,0:T(8,128)(2,1)} async-done(((bf16[16,4096]{1,0:T(8,128)(2,1)}), bf16[256,4096]{1,0:T(8,128)(2,1)}) %all-gather.2.cloned.1.call-update) | async-done | bytes 2097168 | tf_op jit(solution)/shard_map/all_gather | solution.py:40
  68.0 0.0 copy-done.1
  68.0 2.9 %convolution_bitcast_fusion = f32[24,256]{1,0:T(8,128)} fusion(bf16[256,4096]{1,0:T(8,128)(2,1)} %all-gather.2.cloned.1.call-done, bf16[24,4096]{1,0:T(8,128)(2,1)S(1)} %copy-done.1), kind=kOutput, calls=%fused_computation.3 | convolution fusion | flops 50331648 | bytes 2318336 | tf_op jit(solution)/shard_map/dot_general | solution.py:38
  (5 shorter events, 0.1 us)
Async XLA Ops:
  6.5 2.7 %copy-start = (bf16[256,4096]{1,0:T(8,128)(2,1)S(1)}, bf16[256,4096]{1,0:T(8,128)(2,1)}, u32[]{:S(2)}) copy-start(bf16[256,4096]{1,0:T(8,128)(2,1)} %param.7) | copy-start | bytes 6291460
  6.5 61.5 %all-gather.2.cloned.1.call-start = ((), (), s32[]{:S(2)}) async-start(), calls=%async_computation | async-start | bytes 2228224 | tf_op jit(solution)/shard_map/all_gather | solution.py:40
  11.1 56.9 %copy-start.1 = (bf16[24,4096]{1,0:T(8,128)(2,1)S(1)}, bf16[24,4096]{1,0:T(8,128)(2,1)}, u32[]{:S(2)}) copy-start(bf16[24,4096]{1,0:T(8,128)(2,1)} %param.11) | copy-start | bytes 589828
  17.4 6.4 %collective-permute-start = (f32[4096]{0:T(1024)S(1)}, f32[4096]{0:T(1024)S(1)}, u32[]{:S(2)}, u32[]{:S(2)}) collective-permute-start(f32[4096]{0:T(1024)S(1)} %squeeze.7), channel_id=1, source_target_pairs={{0,1},{1,2},{2,3},{3,4},{4,5},{5,6},{6,7},{7,8},{8,9},{9,10},{10,1... | collective-permute-start | bytes 49160 | tf_op jit(solution)/shard_map/ppermute | solution.py:12
Sparse Core Ops, SparseCore 0:
  24.7 43.2 all-gather.1
where the time goes:
time: 78 us; the launch traced here: 77.7 us
  waiting for transfers between devices  44.2 us (57%)
  between operations  13.5 us (17%)
  matrix products  10.9 us (14%)
  starting transfers between devices  4.93 us (6%)
  local copies, waits for them, and re-layouts  2.2 us (3%)
  other arithmetic  2.09 us (3%)
    all_gather x1, waiting for transfers between devices, on_device(): lax.all_gather(owned, ('dp', 'query'), axis=0, tiled=True)  43.5 us
    dot_general x1, matrix products, on_device(): lax.dot_general(spread, in_factor, (((0,), (0,)), ((), ())), preferred_el...  6.18 us
    ppermute x1, starting transfers between devices, passed_along(): return lax.ppermute(x, axis, pairs)  4.93 us
    dot_general x1, matrix products, on_device(): lax.dot_general(query_grads, lax.all_gather(owned, ('dp', 'query'), axis=...  2.87 us
    dot_general x1, matrix products, on_device(): lax.dot_general(out_grad, proj_out, contract, preferred_element_type=jnp....  1.8 us
  transfers between devices with their start and end apart: 2, of which 2 were waited for; matrix products, arithmetic and copies ran while one was open for 1% of the time, Pallas kernels for 0%

commit v1 on v0

v1 whole, which is shorter than its diff:
```python
import functools

import jax
import jax.numpy as jnp
from jax import lax
from jax.experimental import pallas as pl
from jax.experimental.pallas import tpu as pltpu
from jax.sharding import PartitionSpec as P

DOC_DEV = 16
CHUNK = 2048
NT = (((1,), (1,)), ((), ()))
MESH = pl.DeviceIdType.MESH


def dot_nt(a, b):
    return lax.dot_general(a, b, NT, preferred_element_type=jnp.float32)


def kernel(nd, nq, hid, og, ids, pin, pout, q, out,
           hbuf, obuf, pibuf, pobuf, qin, qall, ofb, ifb, gd, sbuf, rbuf,
           hsem, osem, wsem, qs, qr, os_, or_, is_, ir, ss, sr):
    gi, di, qi = lax.axis_index("groups"), lax.axis_index("dp"), lax.axis_index("query")
    rank, tok = ofb.shape[1] - 16, ofb.shape[2]
    rows_q = q.shape[0]
    nh, no = hid.shape[1] // CHUNK, og.shape[1] // CHUNK

    def dp_peer(p):
        return (gi, lax.rem(di + p, nd), qi)

    def query_peer(p):
        return (gi, di, lax.rem(qi + p, nq))

    q_copy = pltpu.make_async_copy(q, qin, wsem.at[0])
    pout_copy = pltpu.make_async_copy(pout, pobuf, wsem.at[1])
    pin_copy = pltpu.make_async_copy(pin, pibuf, wsem.at[2])
    o_copies = [
        pltpu.make_async_copy(og.at[:, pl.ds(c * CHUNK, CHUNK)], obuf.at[:, pl.ds(c * CHUNK, CHUNK)], osem.at[c])
        for c in range(no)
    ]
    h_copies = [
        pltpu.make_async_copy(hid.at[:, pl.ds(c * CHUNK, CHUNK)], hbuf.at[:, pl.ds(c * CHUNK, CHUNK)], hsem.at[c])
        for c in range(nh)
    ]
    q_copy.start()
    pout_copy.start()
    for copy in o_copies:
        copy.start()
    pin_copy.start()
    for copy in h_copies:
        copy.start()

    barrier = pltpu.get_barrier_semaphore()
    for p in range(1, nd):
        pl.semaphore_signal(barrier, inc=1, device_id=dp_peer(p), device_id_type=MESH)
    for p in range(1, nq):
        pl.semaphore_signal(barrier, inc=1, device_id=query_peer(p), device_id_type=MESH)
    pl.semaphore_wait(barrier, nd + nq - 2)

    q_copy.wait()
    half = q.shape[1] // 2
    qv = qin[...].astype(jnp.float32)
    qall[0] = jnp.concatenate([qv[:, :half], qv[:, half:]], axis=0).astype(jnp.bfloat16)

    def remote(src, dst, send, recv, to):
        return pltpu.make_async_remote_copy(
            src_ref=src, dst_ref=dst, send_sem=send, recv_sem=recv, device_id=to, device_id_type=MESH
        )

    q_sends = [remote(qall.at[0], qall.at[p], qs.at[p], qr.at[p], dp_peer(p)) for p in range(1, nd)]
    for copy in q_sends:
        copy.start()

    gd[...] = jnp.zeros_like(gd)
    pout_copy.wait()
    acc = jnp.zeros((rank, tok), jnp.float32)
    for c in range(no):
        o_copies[c].wait()
        cols = pl.ds(c * CHUNK, CHUNK)
        acc += dot_nt(pobuf[:, cols], obuf[:, cols])
    ofb[0, :rank, :] = acc.astype(jnp.bfloat16)
    slot = (ids[...] - (di * nq + qi) * DOC_DEV).astype(jnp.float32)
    ofb[0, rank:, :] = jnp.broadcast_to(slot, (16, tok)).astype(jnp.bfloat16)
    o_sends = [remote(ofb.at[0], ofb.at[p], os_.at[p], or_.at[p], query_peer(p)) for p in range(1, nq)]
    for copy in o_sends:
        copy.start()

    pin_copy.wait()
    acc = jnp.zeros((rank, tok), jnp.float32)
    for c in range(nh):
        h_copies[c].wait()
        cols = pl.ds(c * CHUNK, CHUNK)
        acc += dot_nt(pibuf[:, cols], hbuf[:, cols])
    ifb[0] = acc.astype(jnp.bfloat16)
    i_sends = [remote(ifb.at[0], ifb.at[p], is_.at[p], ir.at[p], query_peer(p)) for p in range(1, nq)]
    for copy in i_sends:
        copy.start()

    eight = (
        lax.broadcasted_iota(jnp.int32, (8 * rank, rank), 0) // 8
        == lax.broadcasted_iota(jnp.int32, (8 * rank, rank), 1)
    ).astype(jnp.float32).astype(jnp.bfloat16)
    low = lax.broadcasted_iota(jnp.int32, (rank // 2, 8, 2 * rank), 2) < rank
    sub = lax.broadcasted_iota(jnp.int32, (8, tok), 0).astype(jnp.float32)
    width = 2 * rank
    for p in range(nq):
        if p:
            o_sends[p - 1].wait_recv()
        of = ofb[p, :rank, :]
        doc = ofb[p, rank:, :].astype(jnp.float32)[:8]
        in_0, in_2 = doc < 8, doc >= 16
        in_1 = jnp.logical_not(jnp.logical_or(in_0, in_2))
        base = jnp.where(in_0, 0.0, jnp.where(in_2, 16.0, 8.0))
        mine = (doc - base == sub).astype(jnp.float32)
        rep = jnp.dot(eight, of, preferred_element_type=jnp.float32)
        a = (rep.reshape(rank, 8, tok) * mine[None]).reshape(8 * rank, tok).astype(jnp.bfloat16)
        if p:
            i_sends[p - 1].wait_recv()
        inf = ifb[p].astype(jnp.float32)
        b0, b1, b2 = (
            jnp.where(jnp.broadcast_to(m[:1], inf.shape), inf, 0.0).astype(jnp.bfloat16) for m in (in_0, in_1, in_2)
        )
        g = dot_nt(a, jnp.concatenate([b0, b1, b1, b0, b2, b2], axis=0))
        g = g.reshape(rank // 2, 16, 3 * width)
        even, odd = g[:, :8, :], g[:, 8:, :]
        g0 = jnp.where(low, even[:, :, :width], odd[:, :, width:2 * width])
        g1 = jnp.where(low, even[:, :, width:2 * width], odd[:, :, :width])
        g2 = jnp.where(low, even[:, :, 2 * width:], odd[:, :, 2 * width:])
        row = pl.multiple_of(lax.rem(qi + nq - p, nq) * DOC_DEV, DOC_DEV)
        gd[:, pl.ds(row, 8), :] += g0
        gd[:, pl.ds(row + 8, 8), :] = g1
        gd[:, pl.ds(row + 16, 8), :] += g2

    for copy in q_sends:
        copy.wait_recv()
    queries = qall[...].reshape(nd * 2 * rows_q, half)
    pairs = rank // 4
    total = []
    for h in range(2):
        docs = jnp.concatenate([gd[h * pairs + m] for m in range(pairs)], axis=1).astype(jnp.bfloat16)
        total.append(dot_nt(queries, docs))
    for p in range(nd):
        at = 2 * p * rows_q
        sbuf[p] = total[0][at:at + rows_q] + total[1][at + rows_q:at + 2 * rows_q]
    s_sends = [remote(sbuf.at[p], rbuf.at[p], ss.at[p], sr.at[p], dp_peer(nd - p)) for p in range(1, nd)]
    for copy in s_sends:
        copy.start()
    rbuf[0] = sbuf[0]
    for copy in s_sends:
        copy.wait_recv()

    per_row = nq * DOC_DEV
    got = [rbuf[lax.rem(r + nd - di, nd)] for r in range(nd)]
    if per_row % 128 == 0:
        for r in range(nd):
            value = got[r][:, :per_row]
            if r:
                value = value + jnp.pad(got[r - 1][:, per_row:per_row + 128], ((0, 0), (0, per_row - 128)))
            out[:, r * per_row:(r + 1) * per_row] = value
    else:
        left = lax.broadcasted_iota(jnp.int32, got[0].shape, 1) < 64
        turned = [pltpu.roll(got[r], 64, 1) if r % 2 else None for r in range(nd)]
        for m in range(nd // 2):
            value = got[2 * m] + jnp.where(left, 0.0, turned[2 * m + 1])
            if m:
                value = value + jnp.where(left, turned[2 * m - 1], 0.0)
            out[:, m * 128:(m + 1) * 128] = value
    for copy in q_sends + o_sends + i_sends + s_sends:
        copy.wait_send()


def solution(mesh):
    nd, nq = mesh.shape["dp"], mesh.shape["query"]

    def on_device(hidden, out_grad, doc_ids, proj_in, proj_out, query_grads):
        tok, ff = hidden.shape
        d = out_grad.shape[1]
        rank = proj_in.shape[0]
        rows_q, flat = query_grads.shape
        per_row = nq * DOC_DEV
        assert rank == 64 and flat == rank * rank and (per_row == 64 or per_row % 128 == 0)
        docs = -(-(per_row + 16) // 128) * 128
        bf16, f32 = jnp.bfloat16, jnp.float32
        dma = pltpu.SemaphoreType.DMA
        hbm = pl.BlockSpec(memory_space=pl.ANY)
        vmem = pl.BlockSpec(memory_space=pltpu.VMEM)
        return pl.pallas_call(
            functools.partial(kernel, nd, nq),
            out_shape=jax.ShapeDtypeStruct((rows_q, nd * per_row), f32),
            in_specs=[hbm, hbm, vmem, hbm, hbm, hbm],
            out_specs=vmem,
            scratch_shapes=[
                pltpu.VMEM((tok, ff), bf16),
                pltpu.VMEM((tok, d), bf16),
                pltpu.VMEM((rank, ff), bf16),
                pltpu.VMEM((rank, d), bf16),
                pltpu.VMEM((rows_q, flat), bf16),
                pltpu.VMEM((nd, 2 * rows_q, flat // 2), bf16),
                pltpu.VMEM((nq, rank + 16, tok), bf16),
                pltpu.VMEM((nq, rank, tok), bf16),
                pltpu.VMEM((rank // 2, docs, 2 * rank), f32),
                pltpu.VMEM((nd, rows_q, docs), f32),
                pltpu.VMEM((nd, rows_q, docs), f32),
                dma((ff // CHUNK,)),
                dma((d // CHUNK,)),
                dma((3,)),
                dma((nd,)),
                dma((nd,)),
                dma((nq,)),
                dma((nq,)),
                dma((nq,)),
                dma((nq,)),
                dma((nd,)),
                dma((nd,)),
            ],
            compiler_params=pltpu.CompilerParams(
                collective_id=0, has_side_effects=True, vmem_limit_bytes=48 * 1024 * 1024
            ),
        )(hidden, out_grad, doc_ids.reshape(1, tok), proj_in, proj_out, query_grads)

    placed = (
        P(("groups", "dp", "query"), None),
        P(("groups", "dp", "query"), None),
        P(("groups", "dp", "query")),
        P(),
        P(),
        P(("dp", "query"), None),
    )
    return jax.shard_map(
        on_device, mesh=mesh, in_specs=placed, out_specs=P(("dp", "query"), "groups"), check_vma=False
    )
```

time: 78 us -> 27.2 us (0.35)
  waiting for transfers between devices: 44.2 us -> 0 us
  Pallas kernels: 0 us -> 20.5 us
  between operations: 13.5 us -> 0.01 us
  matrix products: 10.9 us -> 0 us
  starting transfers between devices: 4.93 us -> 0 us
  local copies, waits for them, and re-layouts: 2.2 us -> 6.35 us
  other arithmetic: 2.09 us -> 0 us
    all_gather x1 -> x0, waiting for transfers between devices: 43.5 us -> none  [on_device(): lax.all_gather(owned, ('dp', 'query'), axis=0, tiled=True)]
    pallas_call x0 -> x1, Pallas kernels: none -> 20.5 us  [on_device(): pl.pallas_call(functools.partial(kernel, nd, nq), out_shape=jax.ShapeDtyp...]
    dot_general x3 -> x0, matrix products: 10.9 us -> none  [the longest x1 6.18 us: on_device(): lax.dot_general(spread, in_factor, (((0,), (0,)), ((), ())), preferred_el...]
    unnamed x4 -> x11, local copies, waits for them, and re-layouts: 0.01 us -> 6.35 us
    ppermute x1 -> x0, starting transfers between devices: 4.93 us -> none  [passed_along(): return lax.ppermute(x, axis, pairs)]
    slice x8 -> x0, local copies, waits for them, and re-layouts: 2.1 us -> none  [the longest x1 1.34 us: on_device(): local_doc = doc_ids - doc_ids[0]]
    sub x1 -> x0, other arithmetic: 1.33 us -> none  [on_device(): local_doc = doc_ids - doc_ids[0]]
  transfers between devices with their start and end apart: 2 -> 0, of which waited for: 2 -> 0; matrix products, arithmetic and copies ran while one was open for 1% -> 0% of each run, Pallas kernels for 0% -> 0%
where the time goes in v1:
time: 27.2 us; the launch traced here: 26.9 us
  Pallas kernels  20.5 us (75%)
  local copies, waits for them, and re-layouts  6.35 us (23%)
    pallas_call x1, Pallas kernels, on_device(): pl.pallas_call(functools.partial(kernel, nd, nq), out_shape=jax.ShapeDtyp...  20.5 us
    unnamed x11, local copies, waits for them, and re-layouts  6.35 us

profile of v1, /device:TPU:0, one launch (start us, length us, event | category | flops | bytes accessed | tf_op | source)
XLA Modules:
  0.0 26.9 jit_solution(7887712140793069113)
XLA Ops:
  0.0 0.0 copy-start
  0.0 1.6 %copy-done = bf16[256,4096]{1,0:T(8,128)(2,1)S(1)} copy-done((bf16[256,4096]{1,0:T(8,128)(2,1)S(1)}, bf16[256,4096]{1,0:T(8,128)(2,1)}, u32[]{:S(2)}) %copy-start) | copy-done | bytes 2097176
  1.6 0.0 copy-start.1
  1.6 1.5 %copy-done.1 = bf16[64,14336]{1,0:T(8,128)(2,1)S(1)} copy-done((bf16[64,14336]{1,0:T(8,128)(2,1)S(1)}, bf16[64,14336]{1,0:T(8,128)(2,1)}, u32[]{:S(2)}) %copy-start.1) | copy-done | bytes 1835032
  3.1 0.0 copy-start.2
  3.1 1.0 %copy-done.2 = bf16[64,4096]{1,0:T(8,128)(2,1)S(1)} copy-done((bf16[64,4096]{1,0:T(8,128)(2,1)S(1)}, bf16[64,4096]{1,0:T(8,128)(2,1)}, u32[]{:S(2)}) %copy-start.2) | copy-done | bytes 524312
  4.1 0.0 copy-start.3
  4.1 0.9 %copy-done.3 = bf16[24,4096]{1,0:T(8,128)(2,1)S(1)} copy-done((bf16[24,4096]{1,0:T(8,128)(2,1)S(1)}, bf16[24,4096]{1,0:T(8,128)(2,1)}, u32[]{:S(2)}) %copy-start.3) | copy-done | bytes 196632
  5.1 0.0 copy-start.4
  5.1 0.7 %copy-done.4 = s32[256]{0:T(256)S(1)} copy-done((s32[256]{0:T(256)S(1)}, s32[256]{0:T(256)}, u32[]{:S(2)}) %copy-start.4) | copy-done | bytes 1048
  5.7 20.5 %shard_map.64 = f32[24,256]{1,0:T(8,128)S(1)} custom-call(bf16[256,14336]{1,0:T(8,128)(2,1)} %hid.1, bf16[256,4096]{1,0:T(8,128)(2,1)S(1)} %copy-done, s32[1,256]{1,0:T(1,128)S(1)} %bitcast.1, bf16[64,14336]{1,0:T(8,128)(2,1)S(1)} %copy-done.1, bf16[64,4096]{1,0:T(8,128)(2,1)S(1)} %copy-done.2, bf16[24,4096]{1,0:T(8,128)(2,1)S(1)} %copy-done.3), custom_call_target="tpu_custom_call" | custom-call | tf_op jit(solution)/shard_map/pallas_call | solution.py:187
  26.3 0.6 %copy.8 = f32[24,256]{1,0:T(8,128)} copy(f32[24,256]{1,0:T(8,128)S(1)} %shard_map.64) | data formatting | bytes 49152
Async XLA Ops:
  0.0 1.6 %copy-start = (bf16[256,4096]{1,0:T(8,128)(2,1)S(1)}, bf16[256,4096]{1,0:T(8,128)(2,1)}, u32[]{:S(2)}) copy-start(bf16[256,4096]{1,0:T(8,128)(2,1)} %og.1) | copy-start | bytes 6291460
  1.6 1.5 %copy-start.1 = (bf16[64,14336]{1,0:T(8,128)(2,1)S(1)}, bf16[64,14336]{1,0:T(8,128)(2,1)}, u32[]{:S(2)}) copy-start(bf16[64,14336]{1,0:T(8,128)(2,1)} %pin.1) | copy-start | bytes 5505028
  3.1 1.0 %copy-start.2 = (bf16[64,4096]{1,0:T(8,128)(2,1)S(1)}, bf16[64,4096]{1,0:T(8,128)(2,1)}, u32[]{:S(2)}) copy-start(bf16[64,4096]{1,0:T(8,128)(2,1)} %pout.1) | copy-start | bytes 1572868
  4.1 0.9 %copy-start.3 = (bf16[24,4096]{1,0:T(8,128)(2,1)S(1)}, bf16[24,4096]{1,0:T(8,128)(2,1)}, u32[]{:S(2)}) copy-start(bf16[24,4096]{1,0:T(8,128)(2,1)} %q.1) | copy-start | bytes 589828
  5.1 0.7 %copy-start.4 = (s32[256]{0:T(256)S(1)}, s32[256]{0:T(256)}, u32[]{:S(2)}) copy-start(s32[256]{0:T(256)} %param.8) | copy-start | bytes 3076

commit v2 on v1

--- a/solution.py
+++ b/solution.py
@@ -18,7 +18,7 @@
 
 
 def kernel(nd, nq, hid, og, ids, pin, pout, q, out,
-           hbuf, obuf, pibuf, pobuf, qin, qall, ofb, ifb, gd, sbuf, rbuf,
+           hbuf, obuf, pibuf, pobuf, idbuf, qin, qall, ofb, ifb, gd, sbuf, rbuf,
            hsem, osem, wsem, qs, qr, os_, or_, is_, ir, ss, sr):
     gi, di, qi = lax.axis_index("groups"), lax.axis_index("dp"), lax.axis_index("query")
     rank, tok = ofb.shape[1] - 16, ofb.shape[2]
@@ -42,7 +42,9 @@
         pltpu.make_async_copy(hid.at[:, pl.ds(c * CHUNK, CHUNK)], hbuf.at[:, pl.ds(c * CHUNK, CHUNK)], hsem.at[c])
         for c in range(nh)
     ]
+    id_copy = pltpu.make_async_copy(ids, idbuf, wsem.at[3])
     q_copy.start()
+    id_copy.start()
     pout_copy.start()
     for copy in o_copies:
         copy.start()
@@ -79,7 +81,8 @@
         cols = pl.ds(c * CHUNK, CHUNK)
         acc += dot_nt(pobuf[:, cols], obuf[:, cols])
     ofb[0, :rank, :] = acc.astype(jnp.bfloat16)
-    slot = (ids[...] - (di * nq + qi) * DOC_DEV).astype(jnp.float32)
+    id_copy.wait()
+    slot = (idbuf[...] - (di * nq + qi) * DOC_DEV).astype(jnp.float32)
     ofb[0, rank:, :] = jnp.broadcast_to(slot, (16, tok)).astype(jnp.bfloat16)
     o_sends = [remote(ofb.at[0], ofb.at[p], os_.at[p], or_.at[p], query_peer(p)) for p in range(1, nq)]
     for copy in o_sends:
@@ -182,18 +185,19 @@
         docs = -(-(per_row + 16) // 128) * 128
         bf16, f32 = jnp.bfloat16, jnp.float32
         dma = pltpu.SemaphoreType.DMA
-        hbm = pl.BlockSpec(memory_space=pl.ANY)
+        hbm = pl.BlockSpec(memory_space=pltpu.HBM)
         vmem = pl.BlockSpec(memory_space=pltpu.VMEM)
         return pl.pallas_call(
             functools.partial(kernel, nd, nq),
             out_shape=jax.ShapeDtypeStruct((rows_q, nd * per_row), f32),
-            in_specs=[hbm, hbm, vmem, hbm, hbm, hbm],
+            in_specs=[hbm] * 6,
             out_specs=vmem,
             scratch_shapes=[
                 pltpu.VMEM((tok, ff), bf16),
                 pltpu.VMEM((tok, d), bf16),
                 pltpu.VMEM((rank, ff), bf16),
                 pltpu.VMEM((rank, d), bf16),
+                pltpu.VMEM((1, tok), jnp.int32),
                 pltpu.VMEM((rows_q, flat), bf16),
                 pltpu.VMEM((nd, 2 * rows_q, flat // 2), bf16),
                 pltpu.VMEM((nq, rank + 16, tok), bf16),
@@ -203,7 +207,7 @@
                 pltpu.VMEM((nd, rows_q, docs), f32),
                 dma((ff // CHUNK,)),
                 dma((d // CHUNK,)),
-                dma((3,)),
+                dma((4,)),
                 dma((nd,)),
                 dma((nd,)),
                 dma((nq,)),
@@ -214,7 +218,7 @@
                 dma((nd,)),
             ],
             compiler_params=pltpu.CompilerParams(
-                collective_id=0, has_side_effects=True, vmem_limit_bytes=48 * 1024 * 1024
+                collective_id=0, has_side_effects=True, vmem_limit_bytes=60 * 1024 * 1024
             ),
         )(hidden, out_grad, doc_ids.reshape(1, tok), proj_in, proj_out, query_grads)
 

time: 27.2 us -> 24.8 us (0.912)
  local copies, waits for them, and re-layouts: 6.35 us -> 1.35 us
  Pallas kernels: 20.5 us -> 23.2 us
    unnamed x11 -> x1, local copies, waits for them, and re-layouts: 6.35 us -> 1.35 us
    pallas_call x1, Pallas kernels: 20.5 us -> 23.2 us  [on_device(): pl.pallas_call(functools.partial(kernel, nd, nq), out_shape=jax.ShapeDtyp...]
where the time goes in v2:
time: 24.8 us; the launch traced here: 24.6 us
  Pallas kernels  23.2 us (94%)
  local copies, waits for them, and re-layouts  1.35 us (5%)
    pallas_call x1, Pallas kernels, on_device(): pl.pallas_call(functools.partial(kernel, nd, nq), out_shape=jax.ShapeDtyp...  23.2 us
    unnamed x1, local copies, waits for them, and re-layouts  1.35 us

profile of v2, /device:TPU:0, one launch (start us, length us, event | category | flops | bytes accessed | tf_op | source)
XLA Modules:
  0.0 24.6 jit_solution(14881973255452867950)
XLA Ops:
  0.0 23.2 %shard_map.64 = f32[24,256]{1,0:T(8,128)} custom-call(bf16[256,14336]{1,0:T(8,128)(2,1)} %hid.1, bf16[256,4096]{1,0:T(8,128)(2,1)} %og.1, s32[1,256]{1,0:T(1,128)} %bitcast.1, bf16[64,14336]{1,0:T(8,128)(2,1)} %pin.1, bf16[64,4096]{1,0:T(8,128)(2,1)} %pout.1, bf16[24,4096]{1,0:T(8,128)(2,1)} %q.1), custom_call_target="tpu_custom_call" | custom-call | tf_op jit(solution)/shard_map/pallas_call | solution.py:190
  23.3 1.3 %copy.8 = f32[24,256]{1,0:T(8,128)} copy(f32[24,256]{1,0:T(8,128)} %shard_map.64) | data formatting | bytes 49152

commit v3 on v2

--- a/solution.py
+++ b/solution.py
@@ -8,22 +8,31 @@
 from jax.sharding import PartitionSpec as P
 
 DOC_DEV = 16
-CHUNK = 2048
+STEP = 256
+O_WIDTHS = (4, 6, 6)
+H_WIDTHS = (8, 8, 10, 14, 16)
 NT = (((1,), (1,)), ((), ()))
 MESH = pl.DeviceIdType.MESH
 
 
+def chunks(total, widths):
+    units, whole = total // STEP, sum(widths)
+    ends = [units * sum(widths[:i + 1]) // whole * STEP for i in range(len(widths))]
+    return [(a, b - a) for a, b in zip([0] + ends[:-1], ends)]
+
+
 def dot_nt(a, b):
     return lax.dot_general(a, b, NT, preferred_element_type=jnp.float32)
 
 
 def kernel(nd, nq, hid, og, ids, pin, pout, q, out,
-           hbuf, obuf, pibuf, pobuf, idbuf, qin, qall, ofb, ifb, gd, sbuf, rbuf,
-           hsem, osem, wsem, qs, qr, os_, or_, is_, ir, ss, sr):
+           hbuf, obuf, pibuf, pobuf, idbuf, qin, qall, ofb, ifb, amask, gd, sbuf, rbuf,
+           hsem, osem, pisem, posem, wsem, qs, qr, os_, or_, is_, ir, ss, sr):
     gi, di, qi = lax.axis_index("groups"), lax.axis_index("dp"), lax.axis_index("query")
     rank, tok = ofb.shape[1] - 16, ofb.shape[2]
     rows_q = q.shape[0]
-    nh, no = hid.shape[1] // CHUNK, og.shape[1] // CHUNK
+    o_cols = chunks(og.shape[1], O_WIDTHS)
+    h_cols = chunks(hid.shape[1], H_WIDTHS)
 
     def dp_peer(p):
         return (gi, lax.rem(di + p, nd), qi)
@@ -31,26 +40,23 @@
     def query_peer(p):
         return (gi, di, lax.rem(qi + p, nq))
 
+    def by_columns(source, target, columns, sems):
+        return [
+            pltpu.make_async_copy(source.at[:, pl.ds(at, n)], target.at[:, pl.ds(at, n)], sems.at[c])
+            for c, (at, n) in enumerate(columns)
+        ]
+
+    po_copies = by_columns(pout, pobuf, o_cols, posem)
+    o_copies = by_columns(og, obuf, o_cols, osem)
+    pi_copies = by_columns(pin, pibuf, h_cols, pisem)
+    h_copies = by_columns(hid, hbuf, h_cols, hsem)
     q_copy = pltpu.make_async_copy(q, qin, wsem.at[0])
-    pout_copy = pltpu.make_async_copy(pout, pobuf, wsem.at[1])
-    pin_copy = pltpu.make_async_copy(pin, pibuf, wsem.at[2])
-    o_copies = [
-        pltpu.make_async_copy(og.at[:, pl.ds(c * CHUNK, CHUNK)], obuf.at[:, pl.ds(c * CHUNK, CHUNK)], osem.at[c])
-        for c in range(no)
-    ]
-    h_copies = [
-        pltpu.make_async_copy(hid.at[:, pl.ds(c * CHUNK, CHUNK)], hbuf.at[:, pl.ds(c * CHUNK, CHUNK)], hsem.at[c])
-        for c in range(nh)
-    ]
-    id_copy = pltpu.make_async_copy(ids, idbuf, wsem.at[3])
+    id_copy = pltpu.make_async_copy(ids, idbuf, wsem.at[1])
     q_copy.start()
     id_copy.start()
-    pout_copy.start()
-    for copy in o_copies:
-        copy.start()
-    pin_copy.start()
-    for copy in h_copies:
-        copy.start()
+    for weight, tokens in zip(po_copies + pi_copies, o_copies + h_copies):
+        weight.start()
+        tokens.start()
 
     barrier = pltpu.get_barrier_semaphore()
     for p in range(1, nd):
@@ -74,11 +80,11 @@
         copy.start()
 
     gd[...] = jnp.zeros_like(gd)
-    pout_copy.wait()
     acc = jnp.zeros((rank, tok), jnp.float32)
-    for c in range(no):
+    for c, (at, n) in enumerate(o_cols):
+        po_copies[c].wait()
         o_copies[c].wait()
-        cols = pl.ds(c * CHUNK, CHUNK)
+        cols = pl.ds(at, n)
         acc += dot_nt(pobuf[:, cols], obuf[:, cols])
     ofb[0, :rank, :] = acc.astype(jnp.bfloat16)
     id_copy.wait()
@@ -88,42 +94,51 @@
     for copy in o_sends:
         copy.start()
 
-    pin_copy.wait()
+    eight = (
+        lax.broadcasted_iota(jnp.int32, (8 * rank, rank), 0) // 8
+        == lax.broadcasted_iota(jnp.int32, (8 * rank, rank), 1)
+    ).astype(jnp.float32).astype(jnp.bfloat16)
+    sub = lax.broadcasted_iota(jnp.int32, (8, tok), 0).astype(jnp.float32)
+
+    def which(p):
+        doc = ofb[p, rank:, :].astype(jnp.float32)[:8]
+        first, past = doc < 8, doc >= 16
+        return doc, first, jnp.logical_not(jnp.logical_or(first, past)), past
+
+    def spread(p):
+        doc, first, _, past = which(p)
+        base = jnp.where(first, 0.0, jnp.where(past, 16.0, 8.0))
+        mine = (doc - base == sub).astype(jnp.float32)
+        rep = jnp.dot(eight, ofb[p, :rank, :], preferred_element_type=jnp.float32)
+        amask[p] = (rep.reshape(rank, 8, tok) * mine[None]).reshape(8 * rank, tok).astype(jnp.bfloat16)
+
+    spread(0)
+
     acc = jnp.zeros((rank, tok), jnp.float32)
-    for c in range(nh):
+    for c, (at, n) in enumerate(h_cols):
+        pi_copies[c].wait()
         h_copies[c].wait()
-        cols = pl.ds(c * CHUNK, CHUNK)
+        cols = pl.ds(at, n)
         acc += dot_nt(pibuf[:, cols], hbuf[:, cols])
     ifb[0] = acc.astype(jnp.bfloat16)
     i_sends = [remote(ifb.at[0], ifb.at[p], is_.at[p], ir.at[p], query_peer(p)) for p in range(1, nq)]
     for copy in i_sends:
         copy.start()
-
-    eight = (
-        lax.broadcasted_iota(jnp.int32, (8 * rank, rank), 0) // 8
-        == lax.broadcasted_iota(jnp.int32, (8 * rank, rank), 1)
-    ).astype(jnp.float32).astype(jnp.bfloat16)
+    for p in range(1, nq):
+        o_sends[p - 1].wait_recv()
+        spread(p)
+
     low = lax.broadcasted_iota(jnp.int32, (rank // 2, 8, 2 * rank), 2) < rank
-    sub = lax.broadcasted_iota(jnp.int32, (8, tok), 0).astype(jnp.float32)
     width = 2 * rank
     for p in range(nq):
         if p:
-            o_sends[p - 1].wait_recv()
-        of = ofb[p, :rank, :]
-        doc = ofb[p, rank:, :].astype(jnp.float32)[:8]
-        in_0, in_2 = doc < 8, doc >= 16
-        in_1 = jnp.logical_not(jnp.logical_or(in_0, in_2))
-        base = jnp.where(in_0, 0.0, jnp.where(in_2, 16.0, 8.0))
-        mine = (doc - base == sub).astype(jnp.float32)
-        rep = jnp.dot(eight, of, preferred_element_type=jnp.float32)
-        a = (rep.reshape(rank, 8, tok) * mine[None]).reshape(8 * rank, tok).astype(jnp.bfloat16)
-        if p:
             i_sends[p - 1].wait_recv()
+        _, in_0, in_1, in_2 = which(p)
         inf = ifb[p].astype(jnp.float32)
         b0, b1, b2 = (
             jnp.where(jnp.broadcast_to(m[:1], inf.shape), inf, 0.0).astype(jnp.bfloat16) for m in (in_0, in_1, in_2)
         )
-        g = dot_nt(a, jnp.concatenate([b0, b1, b1, b0, b2, b2], axis=0))
+        g = dot_nt(amask[p], jnp.concatenate([b0, b1, b1, b0, b2, b2], axis=0))
         g = g.reshape(rank // 2, 16, 3 * width)
         even, odd = g[:, :8, :], g[:, 8:, :]
         g0 = jnp.where(low, even[:, :, :width], odd[:, :, width:2 * width])
@@ -202,12 +217,15 @@
                 pltpu.VMEM((nd, 2 * rows_q, flat // 2), bf16),
                 pltpu.VMEM((nq, rank + 16, tok), bf16),
                 pltpu.VMEM((nq, rank, tok), bf16),
+                pltpu.VMEM((nq, 8 * rank, tok), bf16),
                 pltpu.VMEM((rank // 2, docs, 2 * rank), f32),
                 pltpu.VMEM((nd, rows_q, docs), f32),
                 pltpu.VMEM((nd, rows_q, docs), f32),
-                dma((ff // CHUNK,)),
-                dma((d // CHUNK,)),
-                dma((4,)),
+                dma((len(H_WIDTHS),)),
+                dma((len(O_WIDTHS),)),
+                dma((len(H_WIDTHS),)),
+                dma((len(O_WIDTHS),)),
+                dma((2,)),
                 dma((nd,)),
                 dma((nd,)),
                 dma((nq,)),

time: 24.8 us -> 23.9 us (0.964)
  Pallas kernels: 23.2 us -> 22.4 us
    pallas_call x1, Pallas kernels: 23.2 us -> 22.4 us  [on_device(): pl.pallas_call(functools.partial(kernel, nd, nq), out_shape=jax.ShapeDtyp...]
where the time goes in v3:
time: 23.9 us; the launch traced here: 23.7 us
  Pallas kernels  22.4 us (94%)
  local copies, waits for them, and re-layouts  1.35 us (6%)
    pallas_call x1, Pallas kernels, on_device(): pl.pallas_call(functools.partial(kernel, nd, nq), out_shape=jax.ShapeDtyp...  22.4 us
    unnamed x1, local copies, waits for them, and re-layouts  1.35 us

profile of v3, /device:TPU:0, one launch (start us, length us, event | category | flops | bytes accessed | tf_op | source)
XLA Modules:
  0.0 23.7 jit_solution(3830434023014290023)
XLA Ops:
  0.0 22.4 %shard_map.64 = f32[24,256]{1,0:T(8,128)} custom-call(bf16[256,14336]{1,0:T(8,128)(2,1)} %hid.1, bf16[256,4096]{1,0:T(8,128)(2,1)} %og.1, s32[1,256]{1,0:T(1,128)} %bitcast.1, bf16[64,14336]{1,0:T(8,128)(2,1)} %pin.1, bf16[64,4096]{1,0:T(8,128)(2,1)} %pout.1, bf16[24,4096]{1,0:T(8,128)(2,1)} %q.1), custom_call_target="tpu_custom_call" | custom-call | tf_op jit(solution)/shard_map/pallas_call | solution.py:205
  22.4 1.3 %copy.8 = f32[24,256]{1,0:T(8,128)} copy(f32[24,256]{1,0:T(8,128)} %shard_map.64) | data formatting | bytes 49152

commit v4 on v3

--- a/solution.py
+++ b/solution.py
@@ -79,7 +79,6 @@
     for copy in q_sends:
         copy.start()
 
-    gd[...] = jnp.zeros_like(gd)
     acc = jnp.zeros((rank, tok), jnp.float32)
     for c, (at, n) in enumerate(o_cols):
         po_copies[c].wait()
@@ -144,18 +143,28 @@
         g0 = jnp.where(low, even[:, :, :width], odd[:, :, width:2 * width])
         g1 = jnp.where(low, even[:, :, width:2 * width], odd[:, :, :width])
         g2 = jnp.where(low, even[:, :, 2 * width:], odd[:, :, 2 * width:])
-        row = pl.multiple_of(lax.rem(qi + nq - p, nq) * DOC_DEV, DOC_DEV)
-        gd[:, pl.ds(row, 8), :] += g0
-        gd[:, pl.ds(row + 8, 8), :] = g1
-        gd[:, pl.ds(row + 16, 8), :] += g2
+        gd[p, 0] = g0
+        gd[p, 1] = g1
+        gd[p, 2] = g2
 
     for copy in q_sends:
         copy.wait_recv()
     queries = qall[...].reshape(nd * 2 * rows_q, half)
     pairs = rank // 4
     total = []
+    at_slot = [lax.rem(qi + nq - j, nq) for j in range(nq)]
+    spare = sbuf.shape[2] - nq * DOC_DEV - 8
     for h in range(2):
-        docs = jnp.concatenate([gd[h * pairs + m] for m in range(pairs)], axis=1).astype(jnp.bfloat16)
+        part = pl.ds(h * pairs, pairs)
+        blocks = []
+        for j in range(nq):
+            first = gd[at_slot[j], 0, part]
+            if j:
+                first = first + gd[at_slot[j - 1], 2, part]
+            blocks += [first, gd[at_slot[j], 1, part]]
+        blocks += [gd[at_slot[nq - 1], 2, part], jnp.zeros((pairs, spare, width), jnp.float32)]
+        blocks = jnp.concatenate(blocks, axis=1).astype(jnp.bfloat16)
+        docs = jnp.concatenate([blocks[m] for m in range(pairs)], axis=1)
         total.append(dot_nt(queries, docs))
     for p in range(nd):
         at = 2 * p * rows_q
@@ -218,7 +227,7 @@
                 pltpu.VMEM((nq, rank + 16, tok), bf16),
                 pltpu.VMEM((nq, rank, tok), bf16),
                 pltpu.VMEM((nq, 8 * rank, tok), bf16),
-                pltpu.VMEM((rank // 2, docs, 2 * rank), f32),
+                pltpu.VMEM((nq, 3, rank // 2, 8, 2 * rank), f32),
                 pltpu.VMEM((nd, rows_q, docs), f32),
                 pltpu.VMEM((nd, rows_q, docs), f32),
                 dma((len(H_WIDTHS),)),

time: 23.9 us -> 23.9 us (level)
  no operation moved by 1% of the time
where the time goes in v4:
time: 23.9 us; the launch traced here: 23.7 us
  Pallas kernels  22.4 us (94%)
  local copies, waits for them, and re-layouts  1.35 us (6%)
    pallas_call x1, Pallas kernels, on_device(): pl.pallas_call(functools.partial(kernel, nd, nq), out_shape=jax.ShapeDtyp...  22.4 us
    unnamed x1, local copies, waits for them, and re-layouts  1.35 us

profile of v4, /device:TPU:0, one launch (start us, length us, event | category | flops | bytes accessed | tf_op | source)
XLA Modules:
  0.0 23.7 jit_solution(515806698601908785)
XLA Ops:
  0.0 22.4 %shard_map.64 = f32[24,256]{1,0:T(8,128)} custom-call(bf16[256,14336]{1,0:T(8,128)(2,1)} %hid.1, bf16[256,4096]{1,0:T(8,128)(2,1)} %og.1, s32[1,256]{1,0:T(1,128)} %bitcast.1, bf16[64,14336]{1,0:T(8,128)(2,1)} %pin.1, bf16[64,4096]{1,0:T(8,128)(2,1)} %pout.1, bf16[24,4096]{1,0:T(8,128)(2,1)} %q.1), custom_call_target="tpu_custom_call" | custom-call | tf_op jit(solution)/shard_map/pallas_call | solution.py:214
  22.4 1.3 %copy.8 = f32[24,256]{1,0:T(8,128)} copy(f32[24,256]{1,0:T(8,128)} %shard_map.64) | data formatting | bytes 49152
